TPU v7x, 32 devices: a whole 2x2x4 slice. The times are simulated.
32 devices in a mesh: clip: 2 (over core), fsdp: 16 (over z, y, x).
Axes of the slice: x: 2, y: 2, z: 4, core: 2. Of those that a mesh axis runs over, the one named last changes fastest.
Arguments:
- span_queries: bfloat16 [16, 512, 2560], P('fsdp', None, 'clip'), may hold values from -20 to 20
- span_keys: bfloat16 [16, 512, 2560], P('fsdp', None, 'clip'), may hold values from -12 to 12
- span_values: bfloat16 [16, 512, 2560], P('fsdp', None, 'clip'), may hold values from -6 to 6
- cache_keys: bfloat16 [32, 512, 2560], P(None, 'fsdp', 'clip'), may hold values from -6 to 6
- cache_values: bfloat16 [32, 512, 2560], P(None, 'fsdp', 'clip'), may hold values from -6 to 6
- page_table: int32 [32], replicated, may hold values from 0 to 31, each once
- frame_lists: int32 [16, 6], replicated, may hold values from 0 to 15, as said below
- list_counts: int32 [16], replicated, may hold values from 1 to 6, as said below
- out_weight: bfloat16 [2560, 5120], P('clip', 'fsdp'), may hold values from -1 to 1
Outputs:
- projected: bfloat16 [16, 512, 5120], P('fsdp', 'clip')
Inputs may be any that keep to these rules, and one draw needn't show every extreme that they name: `frame_lists`: each row holds 6 different cached frames; a frame attends to the first list_counts of them. `list_counts`: the counts of frames 2 * i and 2 * i + 1 sum to exactly 7; some frame attends to exactly 6. `page_table`: every block number once.
All inputs are finite; a program needn't handle non-finite values.
Results may differ from a plain program's by a relative error of at most 0.017.
Values may be sent and summed in bfloat16 or wider, within the bound.
A program may use at most 128 MiB of HBM per device.

v0:
```python
import math

import jax
import jax.numpy as jnp
from jax import lax
from jax.sharding import PartitionSpec as P

HD = 128
CF = 8
NC = 16


neg_fill = -1e30


def lookup(values_table, positions):
    table_width = values_table.shape[0]
    matches = positions[..., None] == jnp.arange(table_width, dtype=jnp.int32)
    return jnp.sum(jnp.where(matches, values_table, 0), axis=-1)


def block_numbers(frame_index, slot_index, page_table, frame_lists):
    max_slots = frame_lists.shape[1]
    listed = lookup(frame_lists.reshape(-1), frame_index * max_slots + slot_index)
    return lookup(page_table, frame_index // CF * NC + listed)


def pick_blocks(send_blocks, cache_keys, cache_values):
    slot_total = send_blocks.shape[0]
    frames = send_blocks.shape[1]
    token_slice = cache_keys.shape[1]
    row_width = cache_keys.shape[2]
    sent_keys = cache_keys[send_blocks].reshape(slot_total, frames * token_slice, row_width)
    sent_values = cache_values[send_blocks].reshape(slot_total, frames * token_slice, row_width)
    return (sent_keys, sent_values)


def empty_state(tokens_here, heads_here):
    return (
        jnp.full((tokens_here, heads_here), neg_fill, jnp.float32),
        jnp.zeros((tokens_here, heads_here), jnp.float32),
        jnp.zeros((tokens_here, heads_here, HD), jnp.float32),
    )


def absorb(carried, query_block, key_block, value_block):
    running_max, running_sum, running_out = carried
    scores = jnp.einsum(
        "qhd,khd->qhk", query_block, key_block, preferred_element_type=jnp.float32
    ) * (1.0 / math.sqrt(HD))
    new_max = jnp.maximum(running_max, jnp.max(scores, axis=2))
    shrink = jnp.exp(running_max - new_max)
    weights = jnp.exp(scores - new_max[:, :, None])
    running_sum = running_sum * shrink + jnp.sum(weights, axis=2)
    running_out = running_out * shrink[:, :, None] + jnp.einsum(
        "qhk,khd->qhd",
        weights.astype(jnp.bfloat16),
        value_block,
        preferred_element_type=jnp.float32,
    )
    return (new_max, running_sum, running_out)


def local(
    span_queries,
    span_keys,
    span_values,
    cache_keys,
    cache_values,
    page_table,
    frame_lists,
    list_counts,
    out_weight,
):
    frames = lax.axis_size("fsdp")
    own_frame = lax.axis_index("fsdp")
    tokens_here = span_queries.shape[1]
    row_width = span_queries.shape[2]
    heads_here = row_width // HD
    max_slots = frame_lists.shape[1]
    own_queries = span_queries[0].reshape(tokens_here, heads_here, HD)
    own_keys = span_keys[0].reshape(tokens_here, heads_here, HD)
    own_values = span_values[0].reshape(tokens_here, heads_here, HD)
    destinations = jnp.arange(frames, dtype=jnp.int32)[:, None]
    blank = empty_state(tokens_here, heads_here)
    started = absorb(blank, own_queries, own_keys, own_values)
    slot_index = jnp.arange(max_slots, dtype=jnp.int32)[None, :]
    send_blocks = block_numbers(destinations, slot_index, page_table, frame_lists).T
    sent_keys, sent_values = pick_blocks(send_blocks, cache_keys, cache_values)
    arrived_keys, arrived_values = (
        lax.all_to_all(sent_keys, "fsdp", split_axis=1, concat_axis=1, tiled=True),
        lax.all_to_all(sent_values, "fsdp", split_axis=1, concat_axis=1, tiled=True),
    )
    arrived_keys = arrived_keys.reshape(max_slots, tokens_here, heads_here, HD)
    arrived_values = arrived_values.reshape(max_slots, tokens_here, heads_here, HD)
    item_count = lookup(list_counts, own_frame)

    def advance_own(item_number, carried_one):
        return absorb(
            carried_one, own_queries, arrived_keys[item_number], arrived_values[item_number]
        )

    final_state = lax.fori_loop(0, item_count, advance_own, started)
    running_sum = final_state[1]
    running_out = final_state[2]
    attended = (
        (running_out / running_sum[:, :, None]).astype(jnp.bfloat16).reshape(tokens_here, row_width)
    )
    partial_value = jnp.dot(
        attended,
        lax.all_gather(out_weight, "fsdp", axis=1, tiled=True),
        preferred_element_type=jnp.float32,
    )
    own_rows = lax.psum_scatter(
        partial_value.astype(jnp.bfloat16), "clip", scatter_dimension=0, tiled=True
    )
    return own_rows[None]


def solution(mesh):
    in_specs = (
        P("fsdp", None, "clip"),
        P("fsdp", None, "clip"),
        P("fsdp", None, "clip"),
        P(None, "fsdp", "clip"),
        P(None, "fsdp", "clip"),
        P(),
        P(),
        P(),
        P("clip", "fsdp"),
    )
    out_specs = P("fsdp", "clip", None)
    return jax.shard_map(local, mesh=mesh, in_specs=in_specs, out_specs=out_specs, check_vma=False)
```

profile of v0, /device:TPU:13, one launch (start us, length us, event | category | flops | bytes accessed | tf_op | source)
XLA Modules:
  0.0 737.1 jit_solution(7611325856357710583)
XLA Ops:
  8.8 6.8 gather_fusion
  15.6 11.8 %copy.84 = bf16[6,512,1280]{2,0,1:T(8,128)(2,1)} copy(bf16[6,512,1280]{2,1,0:T(8,128)(2,1)} %bitcast.69) | data formatting | bytes 15728640 | tf_op jit(solution)/shard_map/reshape | solution.py:33
  27.3 6.9 all-to-all-start
  35.0 6.8 gather_fusion.1
  41.8 11.7 %copy.86 = bf16[6,512,1280]{2,0,1:T(8,128)(2,1)} copy(bf16[6,512,1280]{2,1,0:T(8,128)(2,1)} %bitcast.68) | data formatting | bytes 15728640 | tf_op jit(solution)/shard_map/reshape | solution.py:34
  53.5 334.2 %all-to-all-done = bf16[6,512,1280]{2,0,1:T(8,128)(2,1)} async-done(((bf16[6,512,1280]{2,0,1:T(8,128)(2,1)}), bf16[6,512,1280]{2,0,1:T(8,128)(2,1)}, u32[]{:S(2)}, u32[]{:S(2)}) %all-to-all-start) | async-done | bytes 7864352 | tf_op jit(solution)/shard_map/all_to_all | solution.py:91
  387.6 7.2 all-to-all-start.1
  406.0 4.0 bitcast_add_fusion.1
  412.9 14.8 %copy.85 = bf16[6,512,1280]{1,2,0:T(8,128)(2,1)} copy(bf16[6,512,1280]{2,0,1:T(8,128)(2,1)} %all-to-all-done) | data formatting | bytes 15728640 | tf_op jit(solution)/shard_map/all_to_all | solution.py:91
  427.6 200.2 %all-to-all-done.1 = bf16[6,512,1280]{2,0,1:T(8,128)(2,1)} async-done(((bf16[6,512,1280]{2,0,1:T(8,128)(2,1)}), bf16[6,512,1280]{2,0,1:T(8,128)(2,1)}, u32[]{:S(2)}, u32[]{:S(2)}) %all-to-all-start.1) | async-done | bytes 7864352 | tf_op jit(solution)/shard_map/all_to_all | solution.py:92
  627.8 14.8 %copy.87 = bf16[6,512,1280]{1,2,0:T(8,128)(2,1)} copy(bf16[6,512,1280]{2,0,1:T(8,128)(2,1)} %all-to-all-done.1) | data formatting | bytes 15728640 | tf_op jit(solution)/shard_map/all_to_all | solution.py:92
  642.6 49.4 %while.14 = (s32[]{:T(128)}, f32[512,10]{0,1:T(8,128)S(1)}, f32[512,10]{0,1:T(8,128)S(1)}, f32[512,10,128]{0,2,1:T(8,128)S(1)}, s32[]{:T(128)}, /*index=5*/bf16[...) while((s32[]{:T(128)}, f32[512,10]{0,1:T(8,128)S(1)}, ...), condition=%wide.region_8.9_spmd, body=%wide.region_5.8_spmd.sunk | while | flops 1364469760 | bytes 40960152 | solution.py:103
  643.3 3.3 bitcast_reduce_fusion.3
  648.4 4.0 bitcast_add_fusion.3
  653.0 3.3 bitcast_reduce_fusion.3
  658.1 4.0 bitcast_add_fusion.3
  662.7 3.3 bitcast_reduce_fusion.3
  667.8 4.0 bitcast_add_fusion.3
  672.4 3.3 bitcast_reduce_fusion.3
  677.5 4.0 bitcast_add_fusion.3
  682.1 3.3 bitcast_reduce_fusion.3
  687.2 4.0 bitcast_add_fusion.3
  693.5 13.8 %convolution_convert_fusion = bf16[512,5120]{1,0:T(8,128)(2,1)} fusion(bf16[512,1280]{0,1:T(8,128)(2,1)} %bitcast.76, bf16[1280,5120]{0,1:T(8,128)(2,1)} %all-gather.2.cloned.1.call-done), kind=kOutput, calls=%fused_computation.26 | convolution fusion | flops 6713507840 | bytes 19660800 | tf_op jit(solution)/shard_map/dot_general | solution.py:109
  707.4 22.9 %reduce-scatter.2.cloned.1.call-done = bf16[256,5120]{1,0:T(8,128)(2,1)} async-done(((bf16[512,5120]{1,0:T(8,128)(2,1)}), bf16[256,5120]{1,0:T(8,128)(2,1)}) %reduce-scatter.2.cloned.1.call-update) | async-done | bytes 2621456 | tf_op jit(solution)/shard_map/reduce_scatter | solution.py:114
  (57 shorter events, 27.1 us)
Async XLA Ops:
  6.5 2.3 copy-start
  27.3 7.6 %copy-start.2 = (bf16[32,32,1280]{2,1,0:T(8,128)(2,1)S(1)}, bf16[32,32,1280]{2,1,0:T(8,128)(2,1)}, u32[]{:S(2)}) copy-start(bf16[32,32,1280]{2,1,0:T(8,128)(2,1)} %param.15) | copy-start | bytes 7864324
  27.3 360.3 %all-to-all-start = ((bf16[6,512,1280]{2,0,1:T(8,128)(2,1)}), bf16[6,512,1280]{2,0,1:T(8,128)(2,1)}, u32[]{:S(2)}, u32[]{:S(2)}) async-start(bf16[6,512,1280]{2,0,1:T(8,128)(2,1)} %copy.84), calls=%async_computation | async-start | bytes 20971520 | tf_op jit(solution)/shard_map/all_to_all | solution.py:91
  34.2 659.3 %all-gather.2.cloned.1.call-start = ((), (), s32[]{:S(2)}) async-start(), calls=%async_computation.3 | async-start | bytes 13926400 | tf_op jit(solution)/shard_map/all_gather | solution.py:111
  53.5 341.7 %copy-start.3 = (bf16[1,512,1280]{2,1,0:T(8,128)(2,1)S(1)}, bf16[1,512,1280]{2,1,0:T(8,128)(2,1)}, u32[]{:S(2)}) copy-start(bf16[1,512,1280]{2,1,0:T(8,128)(2,1)} %param.11) | copy-start | bytes 3932164
  387.6 240.2 %all-to-all-start.1 = ((bf16[6,512,1280]{2,0,1:T(8,128)(2,1)}), bf16[6,512,1280]{2,0,1:T(8,128)(2,1)}, u32[]{:S(2)}, u32[]{:S(2)}) async-start(bf16[6,512,1280]{2,0,1:T(8,128)(2,1)} %copy.86), calls=%async_computation.1 | async-start | bytes 20971520 | tf_op jit(solution)/shard_map/all_to_all | solution.py:92
  394.9 335.4 %reduce-scatter.2.cloned.1.call-start = ((), (), s32[]{:S(2)}) async-start(), calls=%async_computation.4 | async-start | bytes 7864320 | tf_op jit(solution)/shard_map/reduce_scatter | solution.py:114
  405.9 6.2 copy-start.4
  693.5 36.7 %copy-start.1 = (bf16[32,32,1280]{2,1,0:T(8,128)(2,1)S(1)}, bf16[32,32,1280]{2,1,0:T(8,128)(2,1)}, u32[]{:S(2)}) copy-start(bf16[32,32,1280]{2,1,0:T(8,128)(2,1)} %param.14) | copy-start | bytes 7864324
Sparse Core Ops, SparseCore 0:
  37.8 345.0 all-gather.1
  707.5 22.7 reduce-scatter.1
where the time goes:
time: 740 us; the launch traced here: 737 us
  waiting for transfers between devices  558 us (75%)
  local copies, waits for them, and re-layouts  76 us (10%)
  matrix products  57.1 us (8%)
  starting transfers between devices  14.6 us (2%)
  other arithmetic  13.8 us (2%)
  between operations  13.6 us (2%)
    all_to_all x1, waiting for transfers between devices, local(): lax.all_to_all(sent_keys, 'fsdp', split_axis=1, concat_axis=1, tiled=True)  334 us
    all_to_all x1, waiting for transfers between devices, local(): lax.all_to_all(sent_values, 'fsdp', split_axis=1, concat_axis=1, tiled=True)  200 us
    dot_general x6, matrix products, absorb(): jnp.einsum('qhk,khd->qhd', weights.astype(jnp.bfloat16), value_block, pre...  23.9 us
    reduce_scatter x1, waiting for transfers between devices, local(): lax.psum_scatter(partial_value.astype(jnp.bfloat16), 'clip', scatter_dime...  22.9 us
    dot_general x6, matrix products, absorb(): jnp.einsum('qhd,khd->qhk', query_block, key_block, preferred_element_type...  19.4 us
    all_to_all x1, local copies, waits for them, and re-layouts, local(): lax.all_to_all(sent_values, 'fsdp', split_axis=1, concat_axis=1, tiled=True)  14.8 us
  transfers between devices with their start and end apart: 4, of which 3 were waited for; matrix products, arithmetic and copies ran while one was open for 15% of the time, Pallas kernels for 0%

commit v1 on v0

--- a/solution.py
+++ b/solution.py
@@ -1,13 +1,17 @@
+import functools
 import math
 
 import jax
 import jax.numpy as jnp
 from jax import lax
+from jax.experimental import pallas as pl
+from jax.experimental.pallas import tpu as pltpu
 from jax.sharding import PartitionSpec as P
 
 HD = 128
 CF = 8
 NC = 16
+FT = 512
 
 
 neg_fill = -1e30
@@ -61,7 +65,7 @@
     return (new_max, running_sum, running_out)
 
 
-def local(
+def local_general(
     span_queries,
     span_keys,
     span_values,
@@ -117,6 +121,349 @@
     return own_rows[None]
 
 
+MESH = pl.DeviceIdType.MESH
+LOG2E = 1.4426950408889634
+VMEM_BYTES = 56 * 1024 * 1024
+
+
+def attend_kernel(
+    frames,
+    slots,
+    q_ref,
+    k_ref,
+    v_ref,
+    ck_ref,
+    cv_ref,
+    page_ref,
+    list_ref,
+    count_ref,
+    out_ref,
+    send,
+    recv,
+    qkv,
+    stage,
+    att_in,
+    o_s,
+    m_s,
+    l_s,
+    blk,
+    send_sem,
+    recv_sem,
+    qkv_sem,
+    att_sem,
+):
+    me = lax.axis_index("fsdp")
+    x_me = lax.rem(me, 2)
+    partner = me + 1 - 2 * x_me
+    heads = send.shape[0]
+    half = heads * HD
+    rows = q_ref.shape[0]
+    scale = LOG2E / math.sqrt(HD)
+
+    barrier = pltpu.get_barrier_semaphore()
+
+    def greet(i, carry):
+        pl.semaphore_signal(
+            barrier, inc=1, device_id={"fsdp": lax.rem(me + i, frames)}, device_id_type=MESH
+        )
+        return carry
+
+    lax.fori_loop(1, frames, greet, 0)
+    pl.semaphore_wait(barrier, frames - 1)
+
+    moves = []
+    for t, ref in enumerate((q_ref, k_ref, v_ref)):
+        theirs = pl.multiple_of((1 - x_me) * half, 128)
+        mine = pl.multiple_of(x_me * half, 128)
+        far = pltpu.make_async_remote_copy(
+            src_ref=ref.at[:, pl.ds(theirs, half)],
+            dst_ref=qkv.at[t, x_me],
+            send_sem=qkv_sem.at[0, t],
+            recv_sem=qkv_sem.at[1, t],
+            device_id={"fsdp": partner},
+            device_id_type=MESH,
+        )
+        near = pltpu.make_async_copy(
+            ref.at[:, pl.ds(mine, half)], qkv.at[t, x_me], qkv_sem.at[2, t]
+        )
+        far.start()
+        near.start()
+        moves += [far, near]
+
+    def number(p, carry):
+        first = count_ref[2 * p]
+        for j in range(slots):
+            late = jnp.where(j >= first, 1, 0)
+            at = jnp.minimum(j - late * first, slots - 2)
+            listed = list_ref[2 * p + late, at]
+            blk[p * slots + j] = page_ref[(2 * p) // CF * NC + listed]
+        return carry
+
+    lax.fori_loop(0, frames // 2, number, 0)
+
+    def transfer(h, there, slot):
+        return pltpu.make_async_remote_copy(
+            src_ref=send.at[h, there],
+            dst_ref=recv.at[h, slot],
+            send_sem=send_sem.at[h, there],
+            recv_sem=recv_sem.at[h, slot],
+            device_id={"fsdp": there},
+            device_id_type=MESH,
+        )
+
+    for h in range(heads):
+
+        def fill(i, carry):
+            there = lax.rem(me + i, frames)
+            col = pl.multiple_of(lax.rem(there, 2) * half + h * HD, 128)
+            base = there // 2 * slots
+            for j in range(slots):
+                b = blk[base + j]
+                send[h, there, 0, j] = ck_ref[b, :, pl.ds(col, HD)]
+                send[h, there, 1, j] = cv_ref[b, :, pl.ds(col, HD)]
+            transfer(h, there, me).start()
+            return carry
+
+        lax.fori_loop(1, frames, fill, 0)
+        col = pl.multiple_of(x_me * half + h * HD, 128)
+        for j in range(slots):
+            b = blk[me // 2 * slots + j]
+            recv[h, me, 0, j] = ck_ref[b, :, pl.ds(col, HD)]
+            recv[h, me, 1, j] = cv_ref[b, :, pl.ds(col, HD)]
+
+    for move in moves:
+        move.wait()
+
+    first_me = count_ref[me - x_me]
+
+    def attend(j, q, k, v):
+        s = lax.dot_general(
+            q, k, (((1,), (1,)), ((), ())), preferred_element_type=jnp.float32
+        )
+        top = jnp.max(s, axis=1, keepdims=True)
+        w = jnp.exp2((s - top) * scale)
+        m_s[j] = top
+        l_s[j] = jnp.sum(w, axis=1, keepdims=True)
+        o_s[j] = jnp.dot(w.astype(jnp.bfloat16), v, preferred_element_type=jnp.float32)
+
+    att_moves = []
+    for h in range(heads):
+        cols = slice(h * HD, (h + 1) * HD)
+
+        def own(f, carry):
+            attend(slots + f, qkv[0, f, :, cols], qkv[1, f, :, cols], qkv[2, f, :, cols])
+            return carry
+
+        lax.fori_loop(0, 2, own, 0)
+
+        def arrive(i, carry):
+            there = lax.rem(me + i, frames)
+            transfer(h, there, there).wait_recv()
+            return carry
+
+        lax.fori_loop(1, frames, arrive, 0)
+
+        def listed(j, carry):
+            f = jnp.where(j >= first_me, 1, 0)
+            k = recv[h, :, 0, j].reshape(-1, HD)
+            v = recv[h, :, 1, j].reshape(-1, HD)
+            attend(j, qkv[0, f, :, cols], k, v)
+            return carry
+
+        lax.fori_loop(0, slots, listed, 0)
+
+        for f in range(2):
+
+            def live(j):
+                if j >= slots:
+                    return j - slots == f
+                return (j < first_me) if f == 0 else (j >= first_me)
+
+            tops = [
+                m_s[j]
+                if live(j) is True
+                else jnp.where(live(j), m_s[j], jnp.float32(neg_fill))
+                for j in range(slots + 2)
+                if live(j) is not False
+            ]
+            top = functools.reduce(jnp.maximum, tops)
+            total = jnp.zeros((rows, 1), jnp.float32)
+            summed = jnp.zeros((rows, HD), jnp.float32)
+            at = 0
+            for j in range(slots + 2):
+                if live(j) is False:
+                    continue
+                w = jnp.exp2((tops[at] - top) * scale)
+                at += 1
+                if live(j) is not True:
+                    w = jnp.where(live(j), w, jnp.float32(0))
+                total = total + w * l_s[j]
+                summed = summed + w * o_s[j]
+            stage[h, f] = (summed / total).astype(jnp.bfloat16)
+        move = pltpu.make_async_remote_copy(
+            src_ref=stage.at[h, 1 - x_me],
+            dst_ref=att_in.at[h],
+            send_sem=att_sem.at[0, h],
+            recv_sem=att_sem.at[1, h],
+            device_id={"fsdp": partner},
+            device_id_type=MESH,
+        )
+        move.start()
+        att_moves.append(move)
+        out_ref[:, pl.ds(pl.multiple_of(x_me * half + h * HD, 128), HD)] = stage[h, x_me]
+
+    for h in range(heads):
+        att_moves[h].wait()
+        out_ref[:, pl.ds(pl.multiple_of((1 - x_me) * half + h * HD, 128), HD)] = att_in[h]
+
+    def drain(i, carry):
+        there = lax.rem(me + i, frames)
+        for h in range(heads):
+            transfer(h, there, me).wait_send()
+        return carry
+
+    lax.fori_loop(1, frames, drain, 0)
+
+
+def attend_pair(q, k, v, cache_keys, cache_values, page_table, frame_lists, list_counts, frames):
+    rows, width = q.shape
+    token_slice = cache_keys.shape[1]
+    slots = frame_lists.shape[1] + 1
+    heads = width // HD // 2
+    block = (heads, frames, 2, slots, token_slice, HD)
+    anywhere = pl.BlockSpec(memory_space=pl.ANY)
+    vmem = pl.BlockSpec(memory_space=pltpu.VMEM)
+    smem = pl.BlockSpec(memory_space=pltpu.SMEM)
+    return pl.pallas_call(
+        functools.partial(attend_kernel, frames, slots),
+        out_shape=jax.ShapeDtypeStruct((rows, width), jnp.bfloat16),
+        in_specs=[anywhere] * 3 + [vmem] * 2 + [smem] * 3,
+        out_specs=vmem,
+        scratch_shapes=[
+            pltpu.VMEM(block, jnp.bfloat16),
+            pltpu.VMEM(block, jnp.bfloat16),
+            pltpu.VMEM((3, 2, rows, heads * HD), jnp.bfloat16),
+            pltpu.VMEM((heads, 2, rows, HD), jnp.bfloat16),
+            pltpu.VMEM((heads, rows, HD), jnp.bfloat16),
+            pltpu.VMEM((slots + 2, rows, HD), jnp.float32),
+            pltpu.VMEM((slots + 2, rows, 1), jnp.float32),
+            pltpu.VMEM((slots + 2, rows, 1), jnp.float32),
+            pltpu.SMEM((frames // 2 * slots,), jnp.int32),
+            pltpu.SemaphoreType.DMA((heads, frames)),
+            pltpu.SemaphoreType.DMA((heads, frames)),
+            pltpu.SemaphoreType.DMA((3, 3)),
+            pltpu.SemaphoreType.DMA((2, heads)),
+        ],
+        compiler_params=pltpu.CompilerParams(
+            collective_id=0, has_side_effects=True, vmem_limit_bytes=VMEM_BYTES
+        ),
+        cost_estimate=pl.CostEstimate(
+            flops=4 * rows * rows * HD * heads * (slots + 2),
+            bytes_accessed=64 * 1024 * 1024,
+            transcendentals=rows * rows * heads * (slots + 2),
+        ),
+    )(q, k, v, cache_keys, cache_values, page_table, frame_lists, list_counts)
+
+
+def project_kernel(att_ref, w_ref, out_ref, sent, came, kept, send_sem, recv_sem):
+    step = pl.program_id(0)
+    steps, rows, wide = sent.shape
+    me = lax.axis_index("clip")
+    sibling = 1 - me
+
+    @pl.when(step == 0)
+    def _():
+        barrier = pltpu.get_barrier_semaphore()
+        pl.semaphore_signal(barrier, inc=1, device_id={"clip": sibling}, device_id_type=MESH)
+        pl.semaphore_wait(barrier, 1)
+
+    def move(i):
+        return pltpu.make_async_remote_copy(
+            src_ref=sent.at[i],
+            dst_ref=came.at[i],
+            send_sem=send_sem.at[i],
+            recv_sem=recv_sem.at[i],
+            device_id={"clip": sibling},
+            device_id_type=MESH,
+        )
+
+    def product(half):
+        start = pl.multiple_of(half * rows, rows)
+        return lax.dot_general(
+            att_ref[pl.ds(start, rows), :],
+            w_ref[...],
+            (((1,), (1,)), ((), ())),
+            preferred_element_type=jnp.float32,
+        ).astype(jnp.bfloat16)
+
+    sent[step] = product(sibling)
+    move(step).start()
+    kept[step] = product(me)
+
+    @pl.when(step == steps - 1)
+    def _():
+        for i in range(steps):
+            move(i).wait()
+            out_ref[:, i * wide : (i + 1) * wide] = (
+                kept[i].astype(jnp.float32) + came[i].astype(jnp.float32)
+            ).astype(jnp.bfloat16)
+
+
+def project(attended, weights):
+    columns, depth = weights.shape
+    steps = 4
+    wide = columns // steps
+    rows = attended.shape[0] // 2
+    block = (steps, rows, wide)
+    return pl.pallas_call(
+        project_kernel,
+        grid=(steps,),
+        out_shape=jax.ShapeDtypeStruct((rows, columns), jnp.bfloat16),
+        in_specs=[
+            pl.BlockSpec((2 * rows, depth), lambda i: (0, 0)),
+            pl.BlockSpec((wide, depth), lambda i: (i, 0)),
+        ],
+        out_specs=pl.BlockSpec((rows, columns), lambda i: (0, 0)),
+        scratch_shapes=[
+            pltpu.VMEM(block, jnp.bfloat16),
+            pltpu.VMEM(block, jnp.bfloat16),
+            pltpu.VMEM(block, jnp.bfloat16),
+            pltpu.SemaphoreType.DMA((steps,)),
+            pltpu.SemaphoreType.DMA((steps,)),
+        ],
+        compiler_params=pltpu.CompilerParams(
+            collective_id=1, has_side_effects=True, vmem_limit_bytes=VMEM_BYTES
+        ),
+    )(attended, weights)
+
+
+def local(
+    span_queries,
+    span_keys,
+    span_values,
+    cache_keys,
+    cache_values,
+    page_table,
+    frame_lists,
+    list_counts,
+    out_weight,
+):
+    frames = lax.axis_size("fsdp")
+    attended = attend_pair(
+        span_queries[0],
+        span_keys[0],
+        span_values[0],
+        cache_keys,
+        cache_values,
+        page_table,
+        frame_lists,
+        list_counts,
+        frames,
+    )
+    weights = lax.all_gather(out_weight.T, "fsdp", axis=0, tiled=True)
+    return project(attended, weights)[None]
+
+
 def solution(mesh):
     in_specs = (
         P("fsdp", None, "clip"),
@@ -130,4 +477,7 @@
         P("clip", "fsdp"),
     )
     out_specs = P("fsdp", "clip", None)
-    return jax.shard_map(local, mesh=mesh, in_specs=in_specs, out_specs=out_specs, check_vma=False)
+    clip, fsdp = mesh.shape["clip"], mesh.shape["fsdp"]
+    paired = clip == 2 and fsdp % 4 == 0 and FT // fsdp % 16 == 0
+    body = local if paired else local_general
+    return jax.shard_map(body, mesh=mesh, in_specs=in_specs, out_specs=out_specs, check_vma=False)

time: 740 us -> 380 us (0.51)
  waiting for transfers between devices: 558 us -> 0.73 us
  Pallas kernels: 0 us -> 361 us
  local copies, waits for them, and re-layouts: 76 us -> 4.76 us
  matrix products: 57.1 us -> 0 us
  starting transfers between devices: 14.6 us -> 0.01 us
  other arithmetic: 13.8 us -> 0 us
    all_to_all x2 -> x0, waiting for transfers between devices: 534 us -> none  [the longest x1 334 us: local(): lax.all_to_all(sent_keys, 'fsdp', split_axis=1, concat_axis=1, tiled=True)]
    pallas_call x0 -> x2, Pallas kernels: none -> 361 us  [the longest x1 346 us: attend_pair(): pl.pallas_call(functools.partial(attend_kernel, frames, slots), out_shape...]
    dot_general x13 -> x0, matrix products: 57.1 us -> none  [the longest x6 23.9 us: absorb(): jnp.einsum('qhk,khd->qhd', weights.astype(jnp.bfloat16), value_block, pre...]
    all_to_all x2 -> x0, local copies, waits for them, and re-layouts: 29.6 us -> none  [the longest x1 14.8 us: local(): lax.all_to_all(sent_values, 'fsdp', split_axis=1, concat_axis=1, tiled=True)]
    reshape x3 -> x0, local copies, waits for them, and re-layouts: 23.5 us -> none  [the longest x1 11.8 us: pick_blocks(): cache_keys[send_blocks].reshape(slot_total, frames * token_slice, row_width)]
    reduce_scatter x1 -> x0, waiting for transfers between devices: 22.9 us -> none  [local(): lax.psum_scatter(partial_value.astype(jnp.bfloat16), 'clip', scatter_dime...]
    all_to_all x2 -> x0, starting transfers between devices: 14.1 us -> none  [the longest x1 7.23 us: local(): lax.all_to_all(sent_values, 'fsdp', split_axis=1, concat_axis=1, tiled=True)]
    gather x2 -> x0, local copies, waits for them, and re-layouts: 13.6 us -> none  [the longest x1 6.84 us: pick_blocks(): cache_values[send_blocks]]
  transfers between devices with their start and end apart: 4 -> 1, of which waited for: 3 -> 0; matrix products, arithmetic and copies ran while one was open for 15% -> 0% of each run, Pallas kernels for 0% -> 91%
where the time goes in v1:
time: 380 us
  Pallas kernels  361 us (95%)
  between operations  13.4 us (4%)
  local copies, waits for them, and re-layouts  4.76 us (1%)
    pallas_call x1, Pallas kernels, attend_pair(): pl.pallas_call(functools.partial(attend_kernel, frames, slots), out_shape...  346 us
    pallas_call x1, Pallas kernels, project(): pl.pallas_call(project_kernel, grid=(steps,), out_shape=jax.ShapeDtypeStr...  15.3 us
  transfers between devices with their start and end apart: 1, of which 0 were waited for; matrix products, arithmetic and copies ran while one was open for 0% of the time, Pallas kernels for 91%

profile of v1, /device:TPU:13, one launch (start us, length us, event | category | flops | bytes accessed | tf_op | source)
XLA Modules:
  0.0 379.9 jit_solution(13560309795276124820)
XLA Ops:
  6.5 0.0 all-gather.2.cloned.1.call-start
  6.5 0.7 all-gather.2.cloned.1.call-update
  7.3 1.4 copy.10.list_ref
  8.6 345.7 %shard_map.91.att_ref = bf16[512,1280]{1,0:T(8,128)(2,1)} custom-call(bf16[512,1280]{1,0:T(8,128)(2,1)} %bitcast.7, bf16[512,1280]{1,0:T(8,128)(2,1)} %bitcast.8, bf16[512,1280]{1,0:T(8,128)(2,1)} %bitcast.9, bf16[32,32,1280]{2,1,0:T(8,128)(2,1)} %ck_ref.1, bf16[32,32,1280]{2,1,0:T(8,128)(2,1)} %cv_ref.1, s32[32]{0:T(128)} %page_ref.1, ...), custom_call_target="tpu_custom_call" | custom-call | flops 6039797760 | bytes 67108864 | tf_op jit(solution)/shard_map/pallas_call | solution.py:337
  354.3 0.0 all-gather.2.cloned.1.call-done.w_ref
  354.3 15.3 %shard_map.92 = bf16[256,5120]{1,0:T(8,128)(2,1)} custom-call(bf16[512,1280]{1,0:T(8,128)(2,1)} %shard_map.91.att_ref, bf16[5120,1280]{1,0:T(8,128)(2,1)} %all-gather.2.cloned.1.call-done.w_ref), custom_call_target="tpu_custom_call" | custom-call | tf_op jit(solution)/shard_map/pallas_call | solution.py:418
  369.7 3.4 copy.12
Async XLA Ops:
  6.5 347.8 %all-gather.2.cloned.1.call-start = ((), (), s32[]{:S(2)}) async-start(), calls=%async_computation | async-start | bytes 13926400 | tf_op jit(solution)/shard_map/all_gather | solution.py:463
Sparse Core Ops, SparseCore 0:
  10.1 303.7 all-gather.1

commit v2 on v1

--- a/solution.py
+++ b/solution.py
@@ -137,7 +137,9 @@
     page_ref,
     list_ref,
     count_ref,
+    w_ref,
     out_ref,
+    w_out,
     send,
     recv,
     qkv,
@@ -151,6 +153,7 @@
     recv_sem,
     qkv_sem,
     att_sem,
+    w_sem,
 ):
     me = lax.axis_index("fsdp")
     x_me = lax.rem(me, 2)
@@ -170,6 +173,42 @@
 
     lax.fori_loop(1, frames, greet, 0)
     pl.semaphore_wait(barrier, frames - 1)
+
+    share = w_ref.shape[0]
+
+    def flip(number, bits):
+        for bit in (1, 2, 4, 8):
+            if bits & bit:
+                number = number + bit * (1 - 2 * lax.rem(number // bit, 2))
+        return number
+
+    def pass_on(away, hop):
+        rows_at = pl.ds(pl.multiple_of(flip(me, away) * share, 16), share)
+        return pltpu.make_async_remote_copy(
+            src_ref=w_out.at[rows_at] if away else w_ref,
+            dst_ref=w_out.at[rows_at],
+            send_sem=w_sem.at[0, away ^ hop],
+            recv_sem=w_sem.at[1, away ^ hop],
+            device_id={"fsdp": flip(me, hop)},
+            device_id_type=MESH,
+        )
+
+    passed = []
+
+    def forward(aways, hops):
+        for away in aways:
+            if away:
+                pass_on(away ^ 1, 1).wait_recv()
+        for away in aways:
+            for hop in hops:
+                move = pass_on(away, hop)
+                move.start()
+                passed.append(move)
+
+    own_share = pltpu.make_async_copy(
+        w_ref, w_out.at[pl.ds(pl.multiple_of(me * share, 16), share)], w_sem.at[0, 0]
+    )
+    own_share.start()
 
     moves = []
     for t, ref in enumerate((q_ref, k_ref, v_ref)):
@@ -190,6 +229,8 @@
         near.start()
         moves += [far, near]
 
+    forward([0], [8, 4, 2, 1])
+
     def number(p, carry):
         first = count_ref[2 * p]
         for j in range(slots):
@@ -230,6 +271,10 @@
             b = blk[me // 2 * slots + j]
             recv[h, me, 0, j] = ck_ref[b, :, pl.ds(col, HD)]
             recv[h, me, 1, j] = cv_ref[b, :, pl.ds(col, HD)]
+        if h == 1:
+            forward([8], [4, 2, 1])
+        if h == 2:
+            forward([4, 12], [2, 1])
 
     for move in moves:
         move.wait()
@@ -248,6 +293,8 @@
 
     att_moves = []
     for h in range(heads):
+        if h == 2:
+            forward([1, 9, 5, 13], [2])
         cols = slice(h * HD, (h + 1) * HD)
 
         def own(f, carry):
@@ -316,6 +363,12 @@
         att_moves[h].wait()
         out_ref[:, pl.ds(pl.multiple_of((1 - x_me) * half + h * HD, 128), HD)] = att_in[h]
 
+    own_share.wait()
+    for away in (2, 10, 6, 14, 3, 11, 7, 15):
+        pass_on(away ^ 1, 1).wait_recv()
+    for move in passed:
+        move.wait_send()
+
     def drain(i, carry):
         there = lax.rem(me + i, frames)
         for h in range(heads):
@@ -325,7 +378,9 @@
     lax.fori_loop(1, frames, drain, 0)
 
 
-def attend_pair(q, k, v, cache_keys, cache_values, page_table, frame_lists, list_counts, frames):
+def attend_pair(
+    q, k, v, cache_keys, cache_values, page_table, frame_lists, list_counts, w_rows, frames
+):
     rows, width = q.shape
     token_slice = cache_keys.shape[1]
     slots = frame_lists.shape[1] + 1
@@ -336,9 +391,12 @@
     smem = pl.BlockSpec(memory_space=pltpu.SMEM)
     return pl.pallas_call(
         functools.partial(attend_kernel, frames, slots),
-        out_shape=jax.ShapeDtypeStruct((rows, width), jnp.bfloat16),
-        in_specs=[anywhere] * 3 + [vmem] * 2 + [smem] * 3,
-        out_specs=vmem,
+        out_shape=[
+            jax.ShapeDtypeStruct((rows, width), jnp.bfloat16),
+            jax.ShapeDtypeStruct((frames * w_rows.shape[0], w_rows.shape[1]), jnp.bfloat16),
+        ],
+        in_specs=[anywhere] * 3 + [vmem] * 2 + [smem] * 3 + [anywhere],
+        out_specs=[vmem, anywhere],
         scratch_shapes=[
             pltpu.VMEM(block, jnp.bfloat16),
             pltpu.VMEM(block, jnp.bfloat16),
@@ -353,6 +411,7 @@
             pltpu.SemaphoreType.DMA((heads, frames)),
             pltpu.SemaphoreType.DMA((3, 3)),
             pltpu.SemaphoreType.DMA((2, heads)),
+            pltpu.SemaphoreType.DMA((2, frames)),
         ],
         compiler_params=pltpu.CompilerParams(
             collective_id=0, has_side_effects=True, vmem_limit_bytes=VMEM_BYTES
@@ -362,7 +421,7 @@
             bytes_accessed=64 * 1024 * 1024,
             transcendentals=rows * rows * heads * (slots + 2),
         ),
-    )(q, k, v, cache_keys, cache_values, page_table, frame_lists, list_counts)
+    )(q, k, v, cache_keys, cache_values, page_table, frame_lists, list_counts, w_rows)
 
 
 def project_kernel(att_ref, w_ref, out_ref, sent, came, kept, send_sem, recv_sem):
@@ -449,7 +508,7 @@
     out_weight,
 ):
     frames = lax.axis_size("fsdp")
-    attended = attend_pair(
+    attended, weights = attend_pair(
         span_queries[0],
         span_keys[0],
         span_values[0],
@@ -458,9 +517,9 @@
         page_table,
         frame_lists,
         list_counts,
+        out_weight.T,
         frames,
     )
-    weights = lax.all_gather(out_weight.T, "fsdp", axis=0, tiled=True)
     return project(attended, weights)[None]
 
 
@@ -478,6 +537,6 @@
     )
     out_specs = P("fsdp", "clip", None)
     clip, fsdp = mesh.shape["clip"], mesh.shape["fsdp"]
-    paired = clip == 2 and fsdp % 4 == 0 and FT // fsdp % 16 == 0
+    paired = clip == 2 and fsdp == 16
     body = local if paired else local_general
     return jax.shard_map(body, mesh=mesh, in_specs=in_specs, out_specs=out_specs, check_vma=False)

time: 380 us -> 312 us (0.82)
  Pallas kernels: 361 us -> 307 us
  between operations: 13.4 us -> 0.02 us
    pallas_call x1, Pallas kernels: 346 us -> 292 us  [attend_pair(): pl.pallas_call(functools.partial(attend_kernel, frames, slots), out_shape...]
  transfers between devices with their start and end apart: 1 -> 0, of which waited for: 0 -> 0; matrix products, arithmetic and copies ran while one was open for 0% -> 0% of each run, Pallas kernels for 91% -> 0%
where the time goes in v2:
time: 312 us
  Pallas kernels  307 us (98%)
  local copies, waits for them, and re-layouts  4.76 us (2%)
    pallas_call x1, Pallas kernels, attend_pair(): pl.pallas_call(functools.partial(attend_kernel, frames, slots), out_shape...  292 us
    pallas_call x1, Pallas kernels, project(): pl.pallas_call(project_kernel, grid=(steps,), out_shape=jax.ShapeDtypeStr...  14.8 us

profile of v2, /device:TPU:13, one launch (start us, length us, event | category | flops | bytes accessed | tf_op | source)
XLA Modules:
  0.0 311.6 jit_solution(9439001060873302376)
XLA Ops:
  0.0 1.4 copy.10.list_ref
  1.4 292.0 %shard_map.91 = (bf16[512,1280]{1,0:T(8,128)(2,1)}, bf16[5120,1280]{1,0:T(8,128)(2,1)}) custom-call(bf16[512,1280]{1,0:T(8,128)(2,1)} %bitcast.6, bf16[512,1280]{1,0:T(8,128)(2,1)} %bitcast.7, bf16[512,1280]{1,0:T(8,128)(2,1)} %bitcast.8, bf16[32,32,1280]{2,1,0:T(8,128)(2,1)} %ck_ref.1, bf16[32,32,1280]{2,1,0:T(8,128)(2,1)} %cv_ref.1, s32[32]{0:T(128)} %page_ref.1, ...), custom_call_target="tpu_custom_call" | custom-call | flops 6039797760 | bytes 67108864 | tf_op jit(solution)/shard_map/pallas_call | solution.py:392
  293.4 14.8 %shard_map.92 = bf16[256,5120]{1,0:T(8,128)(2,1)} custom-call(bf16[512,1280]{1,0:T(8,128)(2,1)} %get-tuple-element.7.att_ref, bf16[5120,1280]{1,0:T(8,128)(2,1)} %get-tuple-element.8.w_ref), custom_call_target="tpu_custom_call" | custom-call | tf_op jit(solution)/shard_map/pallas_call | solution.py:477
  308.2 3.4 %copy.12 = bf16[1,256,5120]{2,1,0:T(8,128)(2,1)} copy(bf16[1,256,5120]{2,1,0:T(8,128)(2,1)} %bitcast.5) | data formatting | bytes 5242880

commit v3 on v2

--- a/solution.py
+++ b/solution.py
@@ -255,7 +255,9 @@
     for h in range(heads):
 
         def fill(i, carry):
-            there = lax.rem(me + i, frames)
+            far = lax.rem(i, 2)
+            step = far * (frames // 2) + i // 2
+            there = lax.rem(me + step, frames)
             col = pl.multiple_of(lax.rem(there, 2) * half + h * HD, 128)
             base = there // 2 * slots
             for j in range(slots):
@@ -271,10 +273,13 @@
             b = blk[me // 2 * slots + j]
             recv[h, me, 0, j] = ck_ref[b, :, pl.ds(col, HD)]
             recv[h, me, 1, j] = cv_ref[b, :, pl.ds(col, HD)]
+        if h == 0:
+            forward([8], [4, 2, 1])
         if h == 1:
-            forward([8], [4, 2, 1])
+            forward([4, 12], [2, 1])
         if h == 2:
-            forward([4, 12], [2, 1])
+            forward([1, 9, 5], [2])
+            forward([14], [1])
 
     for move in moves:
         move.wait()
@@ -293,8 +298,6 @@
 
     att_moves = []
     for h in range(heads):
-        if h == 2:
-            forward([1, 9, 5, 13], [2])
         cols = slice(h * HD, (h + 1) * HD)
 
         def own(f, carry):
@@ -364,7 +367,7 @@
         out_ref[:, pl.ds(pl.multiple_of((1 - x_me) * half + h * HD, 128), HD)] = att_in[h]
 
     own_share.wait()
-    for away in (2, 10, 6, 14, 3, 11, 7, 15):
+    for away in (2, 10, 6, 13, 3, 11, 7, 15):
         pass_on(away ^ 1, 1).wait_recv()
     for move in passed:
         move.wait_send()

time: 312 us -> 303 us (0.971); the launches traced: 312 us -> 298 us
  Pallas kernels: 307 us -> 293 us
    pallas_call x1, Pallas kernels: 292 us -> 274 us  [attend_pair(): pl.pallas_call(functools.partial(attend_kernel, frames, slots), out_shape...]
    pallas_call x1, Pallas kernels: 14.8 us -> 18.7 us  [project(): pl.pallas_call(project_kernel, grid=(steps,), out_shape=jax.ShapeDtypeStr...]
where the time goes in v3:
time: 303 us; the launch traced here: 298 us
  Pallas kernels  293 us (97%)
  local copies, waits for them, and re-layouts  4.76 us (2%)
    pallas_call x1, Pallas kernels, attend_pair(): pl.pallas_call(functools.partial(attend_kernel, frames, slots), out_shape...  274 us
    pallas_call x1, Pallas kernels, project(): pl.pallas_call(project_kernel, grid=(steps,), out_shape=jax.ShapeDtypeStr...  18.7 us

profile of v3, /device:TPU:13, one launch (start us, length us, event | category | flops | bytes accessed | tf_op | source)
XLA Modules:
  0.0 297.7 jit_solution(15973924868256048207)
XLA Ops:
  0.0 1.4 copy.10.list_ref
  1.4 274.1 %shard_map.91 = (bf16[512,1280]{1,0:T(8,128)(2,1)}, bf16[5120,1280]{1,0:T(8,128)(2,1)}) custom-call(bf16[512,1280]{1,0:T(8,128)(2,1)} %bitcast.6, bf16[512,1280]{1,0:T(8,128)(2,1)} %bitcast.7, bf16[512,1280]{1,0:T(8,128)(2,1)} %bitcast.8, bf16[32,32,1280]{2,1,0:T(8,128)(2,1)} %ck_ref.1, bf16[32,32,1280]{2,1,0:T(8,128)(2,1)} %cv_ref.1, s32[32]{0:T(128)} %page_ref.1, ...), custom_call_target="tpu_custom_call" | custom-call | flops 6039797760 | bytes 67108864 | tf_op jit(solution)/shard_map/pallas_call | solution.py:395
  275.5 18.7 %shard_map.92 = bf16[256,5120]{1,0:T(8,128)(2,1)} custom-call(bf16[512,1280]{1,0:T(8,128)(2,1)} %get-tuple-element.7.att_ref, bf16[5120,1280]{1,0:T(8,128)(2,1)} %get-tuple-element.8.w_ref), custom_call_target="tpu_custom_call" | custom-call | tf_op jit(solution)/shard_map/pallas_call | solution.py:480
  294.3 3.4 %copy.12 = bf16[1,256,5120]{2,1,0:T(8,128)(2,1)} copy(bf16[1,256,5120]{2,1,0:T(8,128)(2,1)} %bitcast.5) | data formatting | bytes 5242880
